TPU v7x, 256 devices: a whole 4x4x8 slice. The times are simulated.
256 devices in a mesh: hi: 8 (over y_lo, x), lo: 32 (over z, y_hi, core).
Axes of the slice: x: 4, y: 4 (y_hi: 2, y_lo: 2; y = y_hi * 2 + y_lo), z: 8, core: 2. Of those that a mesh axis runs over, the one named last changes fastest.
Arguments:
- density: float32 [16, 1048576], P(None, ('hi', 'lo')), may hold values from -6 to 6
- points: float32 [3, 1048576], P(None, ('hi', 'lo')), may hold values from 0 to 1
- leaf_basis: float32 [8192, 64, 128], P(('hi', 'lo')), may hold values from -0.5 to 0.5
- leaf_interp: float32 [8192, 64, 128], P(('hi', 'lo')), may hold values from -0.75 to 0.75
- translate: float32 [8, 8192, 64, 128], P(None, ('hi', 'lo')), may hold values from -0.5 to 0.5
- offsets: int32 [8192, 4], P(('hi', 'lo')), may hold values from -2 to 2, as said below
- counts: int32 [8192], P(('hi', 'lo')), may hold values from 0 to 4, as said below
Outputs:
- potential: float32 [16, 1048576], P(None, ('hi', 'lo'))
Inputs may be any that keep to these rules, and one draw needn't show every extreme that they name: The 4 offsets of a leaf are distinct; only the first counts entries of a leaf are used. Over the 32 leaves of one device the counts sum to at most 64, and some device reaches that sum in every draw.
All inputs are finite; a program needn't handle non-finite values.
Results may differ from a plain program's by a relative error of at most 0.0003.
Values sent between devices are 32-bit elements; how exact they have to be, the bound alone decides.
A program may use at most 64 MiB of HBM per device.

v0:
```python
import math

import jax
import jax.numpy as jnp
from jax import lax
from jax.sharding import PartitionSpec as P

HIGH = lax.Precision.HIGHEST
SPACING = 0.5
WAVENUM = 3.0
SOFTEN = 0.1
STRENGTH = 0.0625


def from_partner(x, axis, distance):
    return lax.ppermute(x, axis, [(i, i ^ 1 << distance) for i in range(lax.axis_size(axis))])


def padded(cells, sides, width):
    for axis, dim in sides:
        count = lax.axis_size(axis)
        head = lax.slice_in_dim(cells, 0, width, axis=dim)
        tail = lax.slice_in_dim(cells, cells.shape[dim] - width, cells.shape[dim], axis=dim)
        cells = jnp.concatenate(
            [
                lax.ppermute(tail, axis, [(i, (i + 1) % count) for i in range(count)]),
                cells,
                lax.ppermute(head, axis, [((i + 1) % count, i) for i in range(count)]),
            ],
            axis=dim,
        )
    return cells


def kernel_apply(target_pts, source_set, shift_ids, weights):
    dens_rows = source_set.shape[1] - 3
    half_rows = dens_rows // 2
    along = shift_ids.astype(jnp.float32)[:, None, None] * SPACING
    delta_x = along + source_set[:, dens_rows, None, :] - target_pts[:, 0, :, None]
    delta_y = source_set[:, dens_rows + 1, None, :] - target_pts[:, 1, :, None]
    delta_z = source_set[:, dens_rows + 2, None, :] - target_pts[:, 2, :, None]
    distance = jnp.sqrt(delta_x * delta_x + delta_y * delta_y + delta_z * delta_z + SOFTEN * SOFTEN)
    factor = weights[:, None, None] * STRENGTH / distance
    real_part = jnp.cos(WAVENUM * distance) * factor
    imag_part = jnp.sin(WAVENUM * distance) * factor
    source_dens = source_set[:, :dens_rows]
    turned = jnp.concatenate([-source_dens[:, half_rows:], source_dens[:, :half_rows]], axis=1)
    first = jnp.einsum("nab,nrb->nra", real_part, source_dens, precision=HIGH)
    second = jnp.einsum("nab,nrb->nra", imag_part, turned, precision=HIGH)
    return first + second


def near_items(target_all, ext_leaves, pad_leaves, item_leaf, item_shift, item_live):
    item_total = item_leaf.shape[0]
    block_size = math.gcd(item_total, 64)
    groups = item_total // block_size

    def one_block(packed):
        leaf_ids, shift_ids, live_vals = packed
        target_pts = jnp.take(target_all, leaf_ids, axis=0)
        source_set = jnp.take(ext_leaves, leaf_ids + shift_ids + pad_leaves, axis=0)
        return kernel_apply(target_pts, source_set, shift_ids, live_vals)

    result = lax.map(
        one_block,
        (
            item_leaf.reshape(groups, block_size),
            item_shift.reshape(groups, block_size),
            item_live.reshape(groups, block_size),
        ),
    )
    return result.reshape(item_total, result.shape[2], result.shape[3])


def shards(density, points, leaf_basis, leaf_interp, translate, offsets, counts):
    rhs_count, units = density.shape
    rank_size = leaf_basis.shape[1]
    leaf_size = leaf_basis.shape[2]
    leaves = units // leaf_size
    slot_count = offsets.shape[1]
    level_total = translate.shape[0]
    leaf_blocks = density.reshape(rhs_count, leaves, leaf_size)
    state = jnp.einsum("rij,ikj->rik", leaf_blocks, leaf_basis, precision=HIGH)
    lo_top = lax.axis_size("lo").bit_length() - 1
    hi_top = lax.axis_size("hi").bit_length() - 1
    level_plan = []
    for level_idx in range(level_total):
        bit_word = level_idx % (lo_top + hi_top)
        if bit_word < lo_top:
            level_plan.append(("lo", bit_word))
        else:
            level_plan.append(("hi", bit_word - lo_top))
    for level_idx in range(level_total):
        axis_word, bit_pos = level_plan[level_idx]
        flat_state = state.reshape(rhs_count, leaves * rank_size)
        if axis_word == "lo":
            partner = from_partner(flat_state, "lo", bit_pos)
        else:
            partner = from_partner(flat_state, "hi", bit_pos)
        partner = partner.reshape(rhs_count, leaves, rank_size)
        level_mats = translate[level_idx]
        state = jnp.einsum(
            "rik,ikm->rim", state, level_mats[:, :, :rank_size], precision=HIGH
        ) + jnp.einsum("rik,ikm->rim", partner, level_mats[:, :, rank_size:], precision=HIGH)
    far_field = jnp.einsum("rik,ikj->rij", state, leaf_interp, precision=HIGH)
    sources = jnp.concatenate([density, points], axis=0)
    extended = padded(sources, ((("hi", "lo"), 1),), units)
    pad_leaves = units // leaf_size
    ext_leaves = extended.reshape(sources.shape[0], -1, leaf_size).transpose(1, 0, 2)
    target_all = points.reshape(3, leaves, leaf_size).transpose(1, 0, 2)
    slot_ids = jnp.arange(slot_count, dtype=jnp.int32)
    leaf_flat = jnp.repeat(jnp.arange(leaves, dtype=jnp.int32), slot_count)
    shift_flat = offsets.reshape(-1)
    live_flat = (slot_ids[None, :] < counts[:, None]).reshape(-1)
    capacity = leaves * slot_count // 2
    position = jnp.cumsum(live_flat.astype(jnp.int32)) - 1
    target_pos = jnp.where(live_flat, position, capacity)
    item_leaf = (
        jnp.full((capacity,), leaves - 1, jnp.int32).at[target_pos].set(leaf_flat, mode="drop")
    )
    item_shift = jnp.zeros((capacity,), jnp.int32).at[target_pos].set(shift_flat, mode="drop")
    item_live = jnp.zeros((capacity,), jnp.float32).at[target_pos].set(1.0, mode="drop")
    result = near_items(target_all, ext_leaves, pad_leaves, item_leaf, item_shift, item_live)
    near_field = jax.ops.segment_sum(
        result, item_leaf, num_segments=leaves, indices_are_sorted=True
    )
    near_field = near_field.transpose(1, 0, 2)
    return (far_field + near_field).reshape(rhs_count, units)


def solution(mesh):
    return jax.shard_map(
        shards,
        mesh=mesh,
        in_specs=(
            P(None, ("hi", "lo")),
            P(None, ("hi", "lo")),
            P(("hi", "lo"), None, None),
            P(("hi", "lo"), None, None),
            P(None, ("hi", "lo"), None, None),
            P(("hi", "lo"), None),
            P(("hi", "lo")),
        ),
        out_specs=P(None, ("hi", "lo")),
        check_vma=False,
    )
```

profile of v0, /device:TPU:16, one launch (start us, length us, event | category | flops | bytes accessed | tf_op | source)
XLA Modules:
  0.0 192.4 jit_solution(10131731689615266883)
XLA Ops:
  0.0 1.8 constant_dynamic-update-slice_fusion.1
  1.8 1.5 constant_dynamic-update-slice_fusion
  3.7 3.0 %convolution_bitcast_fusion = f32[16,32,64]{2,0,1:T(8,128)S(1)} fusion(f32[32,64,128]{2,1,0:T(8,128)} %param.9, f32[16,4096]{1,0:T(8,128)} %param.7), kind=kOutput, calls=%fused_computation.35 | convolution fusion | flops 50331648 | bytes 1441792 | tf_op jit(solution)/shard_map/rij,ikj->rik/dot_general | solution.py:83
  7.6 3.5 %collective-permute-start = (f32[16,2048]{1,0:T(8,128)}, f32[16,2048]{1,0:T(8,128)}, u32[]{:S(2)}, u32[]{:S(2)}) collective-permute-start(f32[16,2048]{1,0:T(8,128)} %reshape.151), channel_id=1, source_target_pairs={{0,1},{1,0},{2,3},{3,2},{4,5},{5,4},{6,7},{7,6},{8,9},{9,8},{10,11... | collective-permute-start | bytes 393224 | tf_op jit(solution)/shard_map/ppermute | solution.py:16
  15.5 6.3 %slice_bitcast_fusion = (f32[32,64,128]{2,1,0:T(8,128)S(1)}, f32[32,64,128]{2,1,0:T(8,128)}, f32[32,64,128]{2,1,0:T(8,128)}, f32[32,64,128]{2,1,0:T(8,128)}, f32...) fusion(f32[8,32,64,128]{3,2,1,0:T(8,128)} %param.11), kind=kLoop, calls=%fused_computation.76 | loop fusion | bytes 16777216 | tf_op jit(solution)/shard_map/squeeze | solution.py:101
  22.8 1.7 fusion.60
  27.6 1.7 reshape.152
  29.3 2.5 %fusion.37 = f32[16,32,64]{2,0,1:T(8,128)S(1)} fusion(f32[32,16,64]{2,1,0:T(8,128)} %fusion.60, f32[32,64,128]{2,1,0:T(8,128)} %copy-done.1, f32[16,32,64]{2,1,0:T(8,128)} %reshape.152), kind=kOutput, calls=%fused_computation.51 | convolution fusion | flops 25198592 | bytes 1441792 | tf_op jit(solution)/shard_map/rik,ikm->rim/dot_general | solution.py:104
  32.6 1.1 reshape.153
  33.7 6.4 %collective-permute-start.1 = (f32[16,2048]{1,0:T(8,128)S(1)}, f32[16,2048]{1,0:T(8,128)}, u32[]{:S(2)}, u32[]{:S(2)}) collective-permute-start(f32[16,2048]{1,0:T(8,128)S(1)} %reshape.153), channel_id=1, source_target_pairs={{0,2},{1,3},{2,0},{3,1},{4,6},{5,7},{6,4},{7,5},{8,10},{9,11},{10,... | collective-permute-start | bytes 393224 | tf_op jit(solution)/shard_map/ppermute | solution.py:16
  40.0 2.9 %fusion.57 = f32[32,16,64]{2,1,0:T(8,128)} fusion(f32[16,32,64]{2,0,1:T(8,128)S(1)} %fusion.37, f32[32,64,128]{2,1,0:T(8,128)} %get-tuple-element.33), kind=kOutput, calls=%fused_computation.71 | convolution fusion | flops 25165824 | bytes 1310720 | tf_op jit(solution)/shard_map/rik,ikm->rim/dot_general | solution.py:102
  43.0 1.4 collective-permute-done.1
  44.3 1.7 reshape.154
  46.0 2.5 %fusion.36 = f32[16,32,64]{2,0,1:T(8,128)S(1)} fusion(f32[32,16,64]{2,1,0:T(8,128)} %fusion.57, f32[32,64,128]{2,1,0:T(8,128)} %get-tuple-element.33, f32[16,32,64]{2,1,0:T(8,128)} %reshape.154), kind=kOutput, calls=%fused_computation.49 | convolution fusion | flops 25198592 | bytes 1441792 | tf_op jit(solution)/shard_map/rik,ikm->rim/dot_general | solution.py:104
  49.3 1.1 reshape.155
  50.7 2.9 %fusion.54 = f32[32,16,64]{2,1,0:T(8,128)} fusion(f32[16,32,64]{2,0,1:T(8,128)S(1)} %fusion.36, f32[32,64,128]{2,1,0:T(8,128)} %get-tuple-element.32), kind=kOutput, calls=%fused_computation.68 | convolution fusion | flops 25165824 | bytes 1310720 | tf_op jit(solution)/shard_map/rik,ikm->rim/dot_general | solution.py:102
  53.6 1.3 pad_maximum_fusion
  55.2 1.6 copy.100
  56.8 2.8 %gather_fusion = f32[64,19,128]{2,1,0:T(8,128)} fusion(f32[96,19,128]{2,1,0:T(8,128)} %bitcast.75, s32[1024]{0:T(1024)S(1)} %get-tuple-element.46), kind=kCustom, calls=%fused_computation | custom fusion | bytes 1245440 | tf_op jit(solution)/shard_map/while/body/eval_jaxpr/jit(_take)/gather | solution.py:61
  59.6 1.3 broadcast_select_fusion
  61.1 30.0 %fusion = f32[64,16,128]{2,1,0:T(8,128)S(1)} fusion(f32[64,128]{1,0:T(8,128)S(1)} %bitcast.79, f32[64,128]{1,0:T(8,128)S(1)} %bitcast.85, f32[64,128]{1,0:T(8,128)S(1)} %bitcast.81, f32[64,128]{1,0:T(8,128)S(1)} %bitcast.87, f32[64,128]{1,0:T(8,128)S(1)} %bitcast.77, f32[64,128]{1,0:T(8,128)S(1)} %bitcast.83, f32[64]{0:T(128)S(1)} %copy-done.6, ...), kind=kOutput, calls=%fused_computation.6 | convolution fusion | flops 214040576 | bytes 1245440 | tf_op jit(solution)/shard_map/while/body/eval_jaxpr/nab,nrb->nra/dot_general | solution.py:49
  91.1 27.3 %fusion.27 = f32[64,16,128]{2,1,0:T(8,128)} fusion(f32[64,16,128]{2,1,0:T(8,128)S(1)} %fusion, f32[64,128]{1,0:T(8,128)S(1)} %bitcast.80, f32[64,128]{1,0:T(8,128)S(1)} %bitcast.86, f32[64,128]{1,0:T(8,128)S(1)} %bitcast.82, f32[64,128]{1,0:T(8,128)S(1)} %bitcast.88, f32[64,128]{1,0:T(8,128)S(1)} %bitcast.78, f32[64,128]{1,0:T(8,128)S(1)} %bitcast.84, ...), kind=kOutput, calls=%fused_computation.32 | convolution fusion | flops 214040576 | bytes 1769984 | tf_op jit(solution)/shard_map/while/body/eval_jaxpr/nab,nrb->nra/dot_general | solution.py:48
  118.5 1.7 reshape.156
  120.2 2.5 %fusion.35 = f32[16,32,64]{2,0,1:T(8,128)S(1)} fusion(f32[32,16,64]{2,1,0:T(8,128)} %fusion.54, f32[32,64,128]{2,1,0:T(8,128)} %get-tuple-element.32, f32[16,32,64]{2,1,0:T(8,128)} %reshape.156), kind=kOutput, calls=%fused_computation.47 | convolution fusion | flops 25198592 | bytes 1441792 | tf_op jit(solution)/shard_map/rik,ikm->rim/dot_general | solution.py:104
  124.5 2.9 %collective-permute-start.3 = (f32[16,2048]{1,0:T(8,128)S(1)}, f32[16,2048]{1,0:T(8,128)}, u32[]{:S(2)}, u32[]{:S(2)}) collective-permute-start(f32[16,2048]{1,0:T(8,128)S(1)} %reshape.157), channel_id=1, source_target_pairs={{0,8},{1,9},{2,10},{3,11},{4,12},{5,13},{6,14},{7,15},{8,0},{9,1},... | collective-permute-start | bytes 393224 | tf_op jit(solution)/shard_map/ppermute | solution.py:16
  127.5 2.9 %fusion.51 = f32[32,16,64]{2,1,0:T(8,128)} fusion(f32[16,32,64]{2,0,1:T(8,128)S(1)} %fusion.35, f32[32,64,128]{2,1,0:T(8,128)} %get-tuple-element.30), kind=kOutput, calls=%fused_computation.65 | convolution fusion | flops 25165824 | bytes 1310720 | tf_op jit(solution)/shard_map/rik,ikm->rim/dot_general | solution.py:102
  130.4 3.4 %collective-permute-done.3 = f32[16,2048]{1,0:T(8,128)} collective-permute-done((f32[16,2048]{1,0:T(8,128)S(1)}, f32[16,2048]{1,0:T(8,128)}, u32[]{:S(2)}, u32[]{:S(2)}) %collective-permute-start.3) | collective-permute-done | bytes 131104 | tf_op jit(solution)/shard_map/ppermute | solution.py:16
  133.8 1.7 reshape.158
  135.5 2.5 %fusion.34 = f32[16,32,64]{2,0,1:T(8,128)S(1)} fusion(f32[32,16,64]{2,1,0:T(8,128)} %fusion.51, f32[32,64,128]{2,1,0:T(8,128)} %get-tuple-element.30, f32[16,32,64]{2,1,0:T(8,128)} %reshape.158), kind=kOutput, calls=%fused_computation.45 | convolution fusion | flops 25198592 | bytes 1441792 | tf_op jit(solution)/shard_map/rik,ikm->rim/dot_general | solution.py:104
  139.8 4.3 %collective-permute-start.4 = (f32[16,2048]{1,0:T(8,128)S(1)}, f32[16,2048]{1,0:T(8,128)}, u32[]{:S(2)}, u32[]{:S(2)}) collective-permute-start(f32[16,2048]{1,0:T(8,128)S(1)} %reshape.159), channel_id=1, source_target_pairs={{0,16},{1,17},{2,18},{3,19},{4,20},{5,21},{6,22},{7,23},{8,24},{9,... | collective-permute-start | bytes 393224 | tf_op jit(solution)/shard_map/ppermute | solution.py:16
  144.2 2.9 %fusion.48 = f32[32,16,64]{2,1,0:T(8,128)} fusion(f32[16,32,64]{2,0,1:T(8,128)S(1)} %fusion.34, f32[32,64,128]{2,1,0:T(8,128)} %get-tuple-element.28), kind=kOutput, calls=%fused_computation.62 | convolution fusion | flops 25165824 | bytes 1310720 | tf_op jit(solution)/shard_map/rik,ikm->rim/dot_general | solution.py:102
  147.1 2.8 %collective-permute-done.4 = f32[16,2048]{1,0:T(8,128)} collective-permute-done((f32[16,2048]{1,0:T(8,128)S(1)}, f32[16,2048]{1,0:T(8,128)}, u32[]{:S(2)}, u32[]{:S(2)}) %collective-permute-start.4) | collective-permute-done | bytes 131104 | tf_op jit(solution)/shard_map/ppermute | solution.py:16
  149.9 1.7 reshape.160
  151.6 2.5 %fusion.33 = f32[16,32,64]{2,0,1:T(8,128)S(1)} fusion(f32[32,16,64]{2,1,0:T(8,128)} %fusion.48, f32[32,64,128]{2,1,0:T(8,128)} %get-tuple-element.28, f32[16,32,64]{2,1,0:T(8,128)} %reshape.160), kind=kOutput, calls=%fused_computation.43 | convolution fusion | flops 25198592 | bytes 1441792 | tf_op jit(solution)/shard_map/rik,ikm->rim/dot_general | solution.py:104
  156.0 2.8 %collective-permute-start.5 = (f32[16,2048]{1,0:T(8,128)S(1)}, f32[16,2048]{1,0:T(8,128)}, u32[]{:S(2)}, u32[]{:S(2)}) collective-permute-start(f32[16,2048]{1,0:T(8,128)S(1)} %reshape.161), channel_id=1, source_target_pairs={{0,32},{32,0},{64,96},{96,64},{128,160},{160,128},{192,224},{224,1... | collective-permute-start | bytes 393224 | tf_op jit(solution)/shard_map/ppermute | solution.py:16
  158.8 2.9 %fusion.45 = f32[32,16,64]{2,1,0:T(8,128)} fusion(f32[16,32,64]{2,0,1:T(8,128)S(1)} %fusion.33, f32[32,64,128]{2,1,0:T(8,128)} %get-tuple-element.20), kind=kOutput, calls=%fused_computation.59 | convolution fusion | flops 25165824 | bytes 1310720 | tf_op jit(solution)/shard_map/rik,ikm->rim/dot_general | solution.py:102
  161.8 1.7 reshape.162
  163.5 2.5 %fusion.32 = f32[16,32,64]{2,0,1:T(8,128)S(1)} fusion(f32[32,16,64]{2,1,0:T(8,128)} %fusion.45, f32[32,64,128]{2,1,0:T(8,128)} %get-tuple-element.20, f32[16,32,64]{2,1,0:T(8,128)} %reshape.162), kind=kOutput, calls=%fused_computation.41 | convolution fusion | flops 25198592 | bytes 1441792 | tf_op jit(solution)/shard_map/rik,ikm->rim/dot_general | solution.py:104
  166.8 1.1 reshape.163
  167.9 3.6 %collective-permute-start.6 = (f32[16,2048]{1,0:T(8,128)S(1)}, f32[16,2048]{1,0:T(8,128)}, u32[]{:S(2)}, u32[]{:S(2)}) collective-permute-start(f32[16,2048]{1,0:T(8,128)S(1)} %reshape.163), channel_id=1, source_target_pairs={{0,64},{32,96},{64,0},{96,32},{128,192},{160,224},{192,128},{224,1... | collective-permute-start | bytes 393224 | tf_op jit(solution)/shard_map/ppermute | solution.py:16
  171.5 1.7 fusion.42
  173.2 1.3 collective-permute-done.6
  174.6 1.7 reshape.164
  176.3 2.2 %fusion.31 = f32[16,32,64]{2,0,1:T(8,128)S(1)} fusion(f32[32,16,64]{2,1,0:T(8,128)} %fusion.42, f32[32,64,128]{2,1,0:T(8,128)S(1)} %get-tuple-element.35, f32[16,32,64]{2,1,0:T(8,128)} %reshape.164), kind=kOutput, calls=%fused_computation.39 | convolution fusion | flops 25198592 | bytes 1441792 | tf_op jit(solution)/shard_map/rik,ikm->rim/dot_general | solution.py:104
  178.7 1.4 collective-permute-start.7
  181.1 2.7 %collective-permute-done.7 = f32[16,2048]{1,0:T(8,128)S(1)} collective-permute-done((f32[16,2048]{1,0:T(8,128)S(1)}, f32[16,2048]{1,0:T(8,128)S(1)}, u32[]{:S(2)}, u32[]{:S(2)}) %collective-permute-start.7) | collective-permute-done | bytes 131104 | tf_op jit(solution)/shard_map/ppermute | solution.py:16
  183.9 1.2 fusion.30
  186.0 5.6 %scatter_fusion = f32[32,16,128]{2,1,0:T(8,128)S(1)} fusion(f32[32,16,128]{2,1,0:T(8,128)S(1)} %fusion.89, s32[64]{0:T(128)S(1)} %scatter_custom_fusion, f32[64,16,128]{2,1,0:T(8,128)} %fusion.27), kind=kCustom, calls=%fused_computation.5 | custom fusion | flops 131072 | bytes 1573120 | tf_op jit(solution)/shard_map/scatter-add | solution.py:124
  (66 shorter events, 21.5 us)
Async XLA Ops:
  0.0 185.0 %copy-start = (f32[32,64,128]{2,1,0:T(8,128)S(1)}, f32[32,64,128]{2,1,0:T(8,128)}, u32[]{:S(2)}) copy-start(f32[32,64,128]{2,1,0:T(8,128)} %param.10) | copy-start | bytes 3145732
  3.2 50.4 %collective-permute-start.9 = (f32[19,4096]{1,0:T(8,128)}, f32[19,4096]{1,0:T(8,128)}, u32[]{:S(2)}, u32[]{:S(2)}) collective-permute-start(f32[19,4096]{1,0:T(8,128)} %constant_dynamic-update-slice_fusion), channel_id=1, source_target_pairs={{1,0},{2,1},{3,2},{4,3},{5,4},{6,5},{7,6},{8,7},{9,8},{10,9},{11,1... | collective-permute-start | bytes 933896 | tf_op jit(solution)/shard_map/ppermute | solution.py:28
  3.2 50.4 %collective-permute-start.8 = (f32[19,4096]{1,0:T(8,128)}, f32[19,4096]{1,0:T(8,128)}, u32[]{:S(2)}, u32[]{:S(2)}) collective-permute-start(f32[19,4096]{1,0:T(8,128)} %constant_dynamic-update-slice_fusion), channel_id=1, source_target_pairs={{0,1},{1,2},{2,3},{3,4},{4,5},{5,6},{6,7},{7,8},{8,9},{9,10},{10,1... | collective-permute-start | bytes 933896 | tf_op jit(solution)/shard_map/ppermute | solution.py:26
  7.6 20.0 %collective-permute-start = (f32[16,2048]{1,0:T(8,128)}, f32[16,2048]{1,0:T(8,128)}, u32[]{:S(2)}, u32[]{:S(2)}) collective-permute-start(f32[16,2048]{1,0:T(8,128)} %reshape.151), channel_id=1, source_target_pairs={{0,1},{1,0},{2,3},{3,2},{4,5},{5,4},{6,7},{7,6},{8,9},{9,8},{10,11... | collective-permute-start | bytes 393224 | tf_op jit(solution)/shard_map/ppermute | solution.py:16
  15.5 9.1 %copy-start.2 = (f32[3,4096]{1,0:T(4,128)S(1)}, f32[3,4096]{1,0:T(4,128)}, u32[]{:S(2)}) copy-start(f32[3,4096]{1,0:T(4,128)} %param.8) | copy-start | bytes 147460
  21.8 1.0 copy-start.1
  33.7 10.7 %collective-permute-start.1 = (f32[16,2048]{1,0:T(8,128)S(1)}, f32[16,2048]{1,0:T(8,128)}, u32[]{:S(2)}, u32[]{:S(2)}) collective-permute-start(f32[16,2048]{1,0:T(8,128)S(1)} %reshape.153), channel_id=1, source_target_pairs={{0,2},{1,3},{2,0},{3,1},{4,6},{5,7},{6,4},{7,5},{8,10},{9,11},{10,... | collective-permute-start | bytes 393224 | tf_op jit(solution)/shard_map/ppermute | solution.py:16
  50.4 68.1 %collective-permute-start.2 = (f32[16,2048]{1,0:T(8,128)S(1)}, f32[16,2048]{1,0:T(8,128)}, u32[]{:S(2)}, u32[]{:S(2)}) collective-permute-start(f32[16,2048]{1,0:T(8,128)S(1)} %reshape.155), channel_id=1, source_target_pairs={{0,4},{1,5},{2,6},{3,7},{4,0},{5,1},{6,2},{7,3},{8,12},{9,13},{10,... | collective-permute-start | bytes 393224 | tf_op jit(solution)/shard_map/ppermute | solution.py:16
  55.1 6.0 %copy-start.3 = (f32[64,1,128]{2,1,0:T(1,128)S(1)}, f32[64,1,128]{2,1,0:T(1,128)}, u32[]{:S(2)}) copy-start(f32[64,1,128]{2,1,0:T(1,128)} %get-tuple-element.41) | copy-start | bytes 98308
  55.1 6.0 %copy-start.4 = (f32[64,1,128]{2,1,0:T(1,128)S(1)}, f32[64,1,128]{2,1,0:T(1,128)}, u32[]{:S(2)}) copy-start(f32[64,1,128]{2,1,0:T(1,128)} %get-tuple-element.42) | copy-start | bytes 98308
  55.1 6.0 %copy-start.5 = (f32[64,1,128]{2,1,0:T(1,128)S(1)}, f32[64,1,128]{2,1,0:T(1,128)}, u32[]{:S(2)}) copy-start(f32[64,1,128]{2,1,0:T(1,128)} %get-tuple-element.43) | copy-start | bytes 98308
  55.2 6.0 %copy-start.6 = (f32[64]{0:T(128)S(1)}, f32[64]{0:T(128)}, u32[]{:S(2)}) copy-start(f32[64]{0:T(128)} %broadcast_multiply_fusion) | copy-start | bytes 772
  124.5 9.2 %collective-permute-start.3 = (f32[16,2048]{1,0:T(8,128)S(1)}, f32[16,2048]{1,0:T(8,128)}, u32[]{:S(2)}, u32[]{:S(2)}) collective-permute-start(f32[16,2048]{1,0:T(8,128)S(1)} %reshape.157), channel_id=1, source_target_pairs={{0,8},{1,9},{2,10},{3,11},{4,12},{5,13},{6,14},{7,15},{8,0},{9,1},... | collective-permute-start | bytes 393224 | tf_op jit(solution)/shard_map/ppermute | solution.py:16
  139.8 10.1 %collective-permute-start.4 = (f32[16,2048]{1,0:T(8,128)S(1)}, f32[16,2048]{1,0:T(8,128)}, u32[]{:S(2)}, u32[]{:S(2)}) collective-permute-start(f32[16,2048]{1,0:T(8,128)S(1)} %reshape.159), channel_id=1, source_target_pairs={{0,16},{1,17},{2,18},{3,19},{4,20},{5,21},{6,22},{7,23},{8,24},{9,... | collective-permute-start | bytes 393224 | tf_op jit(solution)/shard_map/ppermute | solution.py:16
  156.0 5.8 %collective-permute-start.5 = (f32[16,2048]{1,0:T(8,128)S(1)}, f32[16,2048]{1,0:T(8,128)}, u32[]{:S(2)}, u32[]{:S(2)}) collective-permute-start(f32[16,2048]{1,0:T(8,128)S(1)} %reshape.161), channel_id=1, source_target_pairs={{0,32},{32,0},{64,96},{96,64},{128,160},{160,128},{192,224},{224,1... | collective-permute-start | bytes 393224 | tf_op jit(solution)/shard_map/ppermute | solution.py:16
  167.9 6.7 %collective-permute-start.6 = (f32[16,2048]{1,0:T(8,128)S(1)}, f32[16,2048]{1,0:T(8,128)}, u32[]{:S(2)}, u32[]{:S(2)}) collective-permute-start(f32[16,2048]{1,0:T(8,128)S(1)} %reshape.163), channel_id=1, source_target_pairs={{0,64},{32,96},{64,0},{96,32},{128,192},{160,224},{192,128},{224,1... | collective-permute-start | bytes 393224 | tf_op jit(solution)/shard_map/ppermute | solution.py:16
  178.7 5.1 %collective-permute-start.7 = (f32[16,2048]{1,0:T(8,128)S(1)}, f32[16,2048]{1,0:T(8,128)S(1)}, u32[]{:S(2)}, u32[]{:S(2)}) collective-permute-start(f32[16,2048]{1,0:T(8,128)S(1)} %reshape.165), channel_id=1, source_target_pairs={{0,128},{32,160},{64,192},{96,224},{128,0},{160,32},{192,64},{224,... | collective-permute-start | bytes 393224 | tf_op jit(solution)/shard_map/ppermute | solution.py:16
where the time goes:
time: 195 us; the launch traced here: 192 us
  matrix products  98.7 us (51%)
  local copies, waits for them, and re-layouts  45.9 us (24%)
  starting transfers between devices  25.7 us (13%)
  waiting for transfers between devices  11.8 us (6%)
  other arithmetic  10.1 us (5%)
    dot_general x1, matrix products, kernel_apply(): second = jnp.einsum('nab,nrb->nra', imag_part, turned, precision=HIGH)  30 us
    dot_general x1, matrix products, kernel_apply(): first = jnp.einsum('nab,nrb->nra', real_part, source_dens, precision=HIGH)  27.3 us
    ppermute x8, starting transfers between devices, from_partner(): lax.ppermute(x, axis, [(i, i ^ 1 << distance) for i in range(lax.axis_siz...  25.2 us
    dot_general x8, matrix products, shards(): jnp.einsum('rik,ikm->rim', state, level_mats[:, :, :rank_size], precision...  19 us
    dot_general x8, matrix products, shards(): jnp.einsum('rik,ikm->rim', partner, level_mats[:, :, rank_size:], precisi...  18.3 us
    reshape x8, local copies, waits for them, and re-layouts, shards(): partner = partner.reshape(rhs_count, leaves, rank_size)  12.1 us
    ppermute x8, waiting for transfers between devices, from_partner(): lax.ppermute(x, axis, [(i, i ^ 1 << distance) for i in range(lax.axis_siz...  11.8 us
    reshape x8, local copies, waits for them, and re-layouts, shards(): flat_state = state.reshape(rhs_count, leaves * rank_size)  7.27 us
  transfers between devices with their start and end apart: 10, of which 6 were waited for; matrix products, arithmetic and copies ran while one was open for 59% of the time, Pallas kernels for 0%

commit v1 on v0

v1 whole, which is shorter than its diff:
```python
import functools

import jax
import jax.numpy as jnp
import numpy as np
from jax import lax
from jax.experimental import pallas as pl
from jax.experimental.pallas import tpu as pltpu
from jax.sharding import PartitionSpec as P

MESH = pl.DeviceIdType.MESH
F32 = jnp.float32
BF16 = jnp.bfloat16
SPACING = 0.5
WAVENUM = 3.0
SOFTEN = 0.1
STRENGTH = 0.0625
RHS = 16
LEAF = 128
RANK = 64
PAD = 2
CHUNKS = 4


def fit(func, degree, low, high):
    mid, half = (low + high) / 2, (high - low) / 2
    cheb = np.polynomial.chebyshev.Chebyshev.interpolate(lambda v: func(v * half + mid), degree)
    poly = cheb.convert(kind=np.polynomial.Polynomial).coef
    return [float(c / half**k) for k, c in enumerate(poly)]


T_LOW, T_HIGH = SOFTEN**2 * 0.99, (2 * SPACING + 1) ** 2 + 2 + SOFTEN**2
T_MID = (T_LOW + T_HIGH) / 2
HALF_K = WAVENUM / 2
COS_COEF = fit(lambda t: np.cos(HALF_K * np.sqrt(t)) * np.sqrt(2 * STRENGTH), 6, T_LOW, T_HIGH)
SIN_COEF = fit(lambda t: np.sin(HALF_K * np.sqrt(t)) / np.sqrt(t) * np.sqrt(2 * STRENGTH), 5, T_LOW, T_HIGH)


def horner(coefs, u):
    acc = u * coefs[-1] + coefs[-2]
    for c in coefs[-3::-1]:
        acc = acc * u + c
    return acc


def split2(x):
    hi = x.astype(BF16)
    lo = (x - hi.astype(F32)).astype(BF16)
    return hi, lo


def split3(x):
    a = x.astype(BF16).astype(F32)
    rest = x - a
    b = rest.astype(BF16).astype(F32)
    return a, b, rest - b


def lane_low(shape):
    return lax.broadcasted_iota(jnp.int32, shape, 1) < RANK


def fold(r, rows):
    return r[:rows, :128] + r[:rows, 128:] + r[rows:, :128]


def wide(w):
    hi, lo = split2(w)
    return jnp.concatenate([hi, lo], axis=1)


def tall(x):
    hi, lo = split2(x)
    return jnp.concatenate([hi, lo], axis=0)


def coef_pair(d0, d1, basis):
    x = tall(jnp.concatenate([d0, d1], axis=0))
    r = lax.dot_general(x, tall(basis), (((1,), (1,)), ((), ())), preferred_element_type=F32)
    a = fold(r, 2 * RHS)
    return jnp.where(lane_low((RHS, 128)), a[:RHS], a[RHS:])


def level_pair(own, part, mats):
    x = jnp.concatenate([own, part], axis=0)
    low = lane_low((2 * RHS, 128))
    zero = jnp.zeros_like(x)
    x = tall(jnp.concatenate([jnp.where(low, x, zero), jnp.where(low, zero, x)], axis=0))
    a = fold(jnp.dot(x, wide(mats), preferred_element_type=F32), 4 * RHS)
    own0, part0, own1, part1 = (a[i * RHS : (i + 1) * RHS] for i in range(4))
    low = lane_low((RHS, 128))
    return jnp.where(low, own0, part1) + pltpu.roll(jnp.where(low, own1, part0), RANK, 1)


def interp_pair(state, mats):
    low = lane_low((RHS, 128))
    zero = jnp.zeros_like(state)
    x = tall(jnp.concatenate([jnp.where(low, state, zero), jnp.where(low, zero, state)], axis=0))
    return fold(jnp.dot(x, wide(mats), preferred_element_type=F32), 2 * RHS)


def rows8(*rows):
    index = lax.broadcasted_iota(jnp.int32, (8, LEAF), 0)
    out = jnp.zeros((8, LEAF), F32)
    for i, row in enumerate(rows):
        out = jnp.where(index == i, jnp.broadcast_to(row, (8, LEAF)) if not isinstance(row, float) else row, out)
    return out


def kernel(
    n_hi, n_lo, leaves,
    dens_h, pts_h, basis_h, interp_h, trans_h, off_h, cnt_h, out_ref,
    dens, pts, basis, interp, trans, off, cnt, nxt, halo_d, halo_p, own, part, feat, coords, srcs, items,
    in_sem, basis_sem, trans_sem, send_sem, recv_sem, halo_send, halo_recv,
):
    levels, pairs = trans.shape[0], trans.shape[1]
    per = pairs // CHUNKS
    slots = off.shape[0]
    hi, lo = lax.axis_index("hi"), lax.axis_index("lo")
    flat = hi * n_lo + lo
    total = n_hi * n_lo

    def place(index):
        return (index // n_lo, index % n_lo)

    def partner(bit):
        return place(flat + bit * (1 - 2 * ((flat // bit) % 2)))

    right = place((flat + 1) % total)
    left = place((flat + total - 1) % total)

    barrier = pltpu.get_barrier_semaphore()
    for level in range(levels):
        pl.semaphore_signal(barrier, inc=1, device_id=partner(1 << level), device_id_type=MESH)
    for side in (left, right):
        pl.semaphore_signal(barrier, inc=1, device_id=side, device_id_type=MESH)

    load_dens = pltpu.make_async_copy(dens_h, dens, in_sem.at[0])
    load_pts = pltpu.make_async_copy(pts_h, pts, in_sem.at[1])
    load_off = pltpu.make_async_copy(off_h, off, in_sem.at[2])
    load_cnt = pltpu.make_async_copy(cnt_h, cnt, in_sem.at[3])
    load_interp = pltpu.make_async_copy(interp_h, interp, in_sem.at[4])
    load_basis = [
        pltpu.make_async_copy(basis_h.at[pl.ds(c * per, per)], basis.at[pl.ds(c * per, per)], basis_sem.at[c])
        for c in range(CHUNKS)
    ]

    def load_trans(level):
        return pltpu.make_async_copy(trans_h.at[level], trans.at[level], trans_sem.at[level])

    load_dens.start()
    for copy in load_basis:
        copy.start()
    load_trans(0).start()
    load_pts.start()
    load_off.start()
    load_cnt.start()
    for level in range(1, levels):
        load_trans(level).start()
    load_interp.start()

    def send(level, chunk, target):
        return pltpu.make_async_remote_copy(
            src_ref=own.at[level, pl.ds(chunk * per, per)],
            dst_ref=part.at[level, pl.ds(chunk * per, per)],
            send_sem=send_sem.at[level, chunk],
            recv_sem=recv_sem.at[level, chunk],
            device_id=target,
            device_id_type=MESH,
        )

    halo_copies = []
    edge = (leaves - PAD) * LEAF
    for i, (start, side, target) in enumerate(((edge, 0, right), (0, 1, left))):
        for j, (src, dst) in enumerate(((dens, halo_d), (pts, halo_p))):
            halo_copies.append(
                pltpu.make_async_remote_copy(
                    src_ref=src.at[:, pl.ds(start, PAD * LEAF)],
                    dst_ref=dst.at[side],
                    send_sem=halo_send.at[2 * i + j],
                    recv_sem=halo_recv.at[2 * i + j],
                    device_id=target,
                    device_id_type=MESH,
                )
            )

    load_dens.wait()
    for c in range(CHUNKS):
        load_basis[c].wait()

        def coef_step(i, _, c=c):
            p = c * per + i
            base = pl.multiple_of(p * 2 * LEAF, 2 * LEAF)
            block = dens[:, pl.ds(base, 2 * LEAF)]
            own[0, p] = coef_pair(block[:, :LEAF], block[:, LEAF:], basis[p])
            return 0

        lax.fori_loop(0, per, coef_step, 0, unroll=True)
    load_pts.wait()
    pl.semaphore_wait(barrier, levels + 2)
    for c in range(CHUNKS):
        send(0, c, partner(1)).start()
    for copy in halo_copies:
        copy.start()

    def level_task(level, chunk):
        for i in range(per):
            p = chunk * per + i
            own[level + 1, p] = level_pair(own[level, p], part[level, p], trans[level, p])

    load_trans(0).wait()

    def first_task(chunk, _):
        send(0, chunk, partner(1)).wait()
        level_task(0, chunk)
        send(1, chunk, partner(2)).start()
        return 0

    lax.fori_loop(0, CHUNKS, first_task, 0)

    def prepare(e, d, p):
        turned = jnp.concatenate([-d[RHS // 2 :], d[: RHS // 2]], axis=0)
        srcs[e] = tall(jnp.concatenate([d, turned], axis=1))
        x, y, z = (p[k : k + 1] - 0.5 for k in range(3))
        rows = rows8(x, y, z, x * x + y * y + z * z, 1.0)
        coords[e] = rows
        a, b, c = split3(rows)
        feat[e] = jnp.concatenate([a, a, b, b, a, c], axis=0).T.astype(BF16)

    def prepare_own(q, _):
        base = pl.multiple_of(q * LEAF, LEAF)
        prepare(q + PAD, dens[:, pl.ds(base, LEAF)], pts[:, pl.ds(base, LEAF)])
        return 0

    lax.fori_loop(0, leaves, prepare_own, 0, unroll=2)
    load_off.wait()
    load_cnt.wait()

    def link_step(i, following):
        q = leaves - 1 - i
        nxt[q + 1] = following
        return jnp.where(cnt[q] > 0, q, following)

    first_leaf = lax.fori_loop(0, leaves, link_step, jnp.int32(leaves - 1))
    for copy in halo_copies:
        copy.wait()
    for side in range(2):
        for i in range(PAD):
            e = side * (leaves + PAD) + i
            prepare(e, halo_d[side, :, i * LEAF : (i + 1) * LEAF], halo_p[side, :, i * LEAF : (i + 1) * LEAF])

    def item(j, leaf, slot, acc):
        shift = off[jnp.minimum(slot, slots - 1), leaf]
        source = leaf + shift + PAD
        p = coords[leaf + PAD]
        x = p[0:1] - SPACING * shift.astype(F32)
        y, z = p[1:2], p[2:3]
        rows = rows8(-2 * x, -2 * y, -2 * z, 1.0, x * x + y * y + z * z + SOFTEN * SOFTEN)
        a, b, c = split3(rows)
        target = jnp.concatenate([a, b, a, b, c, a], axis=0).astype(BF16)
        t = jnp.dot(feat[source], target, preferred_element_type=F32)
        u = t - T_MID
        cosine = horner(COS_COEF, u)
        real = (cosine * cosine - STRENGTH) * lax.rsqrt(t)
        imag = horner(SIN_COEF, u) * cosine
        mats = jnp.concatenate([wide(real), wide(imag)], axis=0)
        r = fold(jnp.dot(srcs[source], mats, preferred_element_type=F32), RHS)
        acc = r + jnp.where(slot == 0, 0.0, acc)
        items[j] = acc
        slot = slot + 1
        done = slot >= cnt[leaf]
        return jnp.where(done, nxt[leaf + 1], leaf), jnp.where(done, 0, slot), acc

    def unit(k, carry):
        leaf, slot, acc = carry
        for i in range(2):
            leaf, slot, acc = item(2 * k + i, leaf, slot, acc)
        return leaf, slot, acc

    units = items.shape[0] // 2
    every = units // ((levels - 1) * CHUNKS)
    spare = units - every * (levels - 1) * CHUNKS
    carry = (first_leaf, jnp.int32(0), jnp.zeros((RHS, LEAF), F32))
    carry = lax.fori_loop(0, spare, unit, carry)

    def middle_level(level, state):
        bit, carry = state
        load_trans(level).wait()

        def task(chunk, carry):
            start = spare + ((level - 1) * CHUNKS + chunk) * every
            carry = lax.fori_loop(start, start + every, unit, carry)
            send(level, chunk, partner(bit)).wait()
            level_task(level, chunk)
            send(level + 1, chunk, partner(bit * 2)).start()
            return carry

        return bit * 2, lax.fori_loop(0, CHUNKS, task, carry)

    bit, carry = lax.fori_loop(1, levels - 1, middle_level, (jnp.int32(2), carry))
    last = levels - 1
    for chunk in range(CHUNKS):
        start = spare + ((last - 1) * CHUNKS + chunk) * every
        carry = lax.fori_loop(start, start + every, unit, carry)
    load_trans(last).wait()
    load_interp.wait()

    def last_task(chunk, end):
        send(last, chunk, partner(1 << last)).wait()
        level_task(last, chunk)
        for i in range(per):
            p = chunk * per + i
            far = interp_pair(own[levels, p], interp[p])
            for h in range(2):
                q = 2 * p + h
                count = cnt[q]
                end = end + count
                near = jnp.where(count > 0, items[jnp.maximum(end - 1, 0)], 0.0)
                out_ref[:, pl.ds(pl.multiple_of(q * LEAF, LEAF), LEAF)] = far[h * RHS : (h + 1) * RHS] + near
        return end

    lax.fori_loop(0, CHUNKS, last_task, jnp.int32(0))


def solution(mesh):
    n_hi, n_lo = mesh.shape["hi"], mesh.shape["lo"]

    def shards(density, points, leaf_basis, leaf_interp, translate, offsets, counts):
        leaves = leaf_basis.shape[0]
        levels = translate.shape[0]
        pairs = leaves // 2
        ext = leaves + 2 * PAD
        capacity = leaves * offsets.shape[1] // 2
        any_spec = pl.BlockSpec(memory_space=pl.ANY)
        dma = pltpu.SemaphoreType.DMA
        return pl.pallas_call(
            functools.partial(kernel, n_hi, n_lo, leaves),
            out_shape=jax.ShapeDtypeStruct(density.shape, F32),
            in_specs=[any_spec] * 7,
            out_specs=pl.BlockSpec(memory_space=pltpu.VMEM),
            scratch_shapes=[
                pltpu.VMEM(density.shape, F32),
                pltpu.VMEM(points.shape, F32),
                pltpu.VMEM((pairs, 128, 128), F32),
                pltpu.VMEM((pairs, 128, 128), F32),
                pltpu.VMEM((levels, pairs, 128, 128), F32),
                pltpu.SMEM(offsets.shape[::-1], jnp.int32),
                pltpu.SMEM(counts.shape, jnp.int32),
                pltpu.SMEM((leaves + 1,), jnp.int32),
                pltpu.VMEM((2, RHS, PAD * LEAF), F32),
                pltpu.VMEM((2, 3, PAD * LEAF), F32),
                pltpu.VMEM((levels + 1, pairs, RHS, 128), F32),
                pltpu.VMEM((levels, pairs, RHS, 128), F32),
                pltpu.VMEM((ext, LEAF, 48), BF16),
                pltpu.VMEM((ext, 8, LEAF), F32),
                pltpu.VMEM((ext, 2 * RHS, 2 * LEAF), BF16),
                pltpu.VMEM((capacity, RHS, LEAF), F32),
                dma((5,)),
                dma((CHUNKS,)),
                dma((levels,)),
                dma((levels, CHUNKS)),
                dma((levels, CHUNKS)),
                dma((4,)),
                dma((4,)),
            ],
            compiler_params=pltpu.CompilerParams(
                collective_id=0, has_side_effects=True, vmem_limit_bytes=60 << 20
            ),
            name="helmholtz",
        )(
            density,
            points,
            leaf_basis.reshape(pairs, 2 * RANK, LEAF),
            leaf_interp.reshape(pairs, 2 * RANK, LEAF),
            translate.reshape(levels, pairs, 2 * RANK, 2 * RANK),
            offsets.T,
            counts,
        )

    return jax.shard_map(
        shards,
        mesh=mesh,
        in_specs=(
            P(None, ("hi", "lo")),
            P(None, ("hi", "lo")),
            P(("hi", "lo"), None, None),
            P(("hi", "lo"), None, None),
            P(None, ("hi", "lo"), None, None),
            P(("hi", "lo"), None),
            P(("hi", "lo")),
        ),
        out_specs=P(None, ("hi", "lo")),
        check_vma=False,
    )
```

time: 195 us -> 50 us (0.26); the launches traced: 192 us -> 49.9 us
  matrix products: 98.7 us -> 0 us
  Pallas kernels: 0 us -> 48.2 us
  local copies, waits for them, and re-layouts: 45.9 us -> 1.67 us
  starting transfers between devices: 25.7 us -> 0 us
  waiting for transfers between devices: 11.8 us -> 0 us
  other arithmetic: 10.1 us -> 0 us
    dot_general x20 -> x0, matrix products: 98.7 us -> none  [the longest x1 30 us: kernel_apply(): second = jnp.einsum('nab,nrb->nra', imag_part, turned, precision=HIGH)]
    pallas_call x0 -> x1, Pallas kernels: none -> 48.2 us  [shards(): pl.pallas_call(functools.partial(kernel, n_hi, n_lo, leaves), out_shape=j...]
    ppermute x10 -> x0, starting transfers between devices: 25.7 us -> none  [the longest x8 25.2 us: from_partner(): lax.ppermute(x, axis, [(i, i ^ 1 << distance) for i in range(lax.axis_siz...]
    reshape x21 -> x0, local copies, waits for them, and re-layouts: 21.9 us -> none  [the longest x8 12.1 us: shards(): partner = partner.reshape(rhs_count, leaves, rank_size)]
    ppermute x10 -> x0, waiting for transfers between devices: 11.8 us -> none  [the longest x8 11.8 us: from_partner(): lax.ppermute(x, axis, [(i, i ^ 1 << distance) for i in range(lax.axis_siz...]
    squeeze x1 -> x0, local copies, waits for them, and re-layouts: 6.33 us -> none  [shards(): level_mats = translate[level_idx]]
    scatter-add x1 -> x0, other arithmetic: 5.64 us -> none  [shards(): jax.ops.segment_sum(result, item_leaf, num_segments=leaves, indices_are_s...]
    add x7 -> x0, local copies, waits for them, and re-layouts: 4.8 us -> none  [shards(): jnp.einsum('rik,ikm->rim', state, level_mats[:, :, :rank_size], precision...]
  transfers between devices with their start and end apart: 10 -> 0, of which waited for: 6 -> 0; matrix products, arithmetic and copies ran while one was open for 59% -> 0% of each run, Pallas kernels for 0% -> 0%
where the time goes in v1:
time: 50 us; the launch traced here: 49.9 us
  Pallas kernels  48.2 us (96%)
  local copies, waits for them, and re-layouts  1.67 us (3%)
    pallas_call x1, Pallas kernels, shards(): pl.pallas_call(functools.partial(kernel, n_hi, n_lo, leaves), out_shape=j...  48.2 us
    unnamed x1, local copies, waits for them, and re-layouts  1.67 us

profile of v1, /device:TPU:16, one launch (start us, length us, event | category | flops | bytes accessed | tf_op | source)
XLA Modules:
  0.0 49.9 jit_solution(6015489393756811348)
XLA Ops:
  0.0 48.2 %helmholtz.1 = f32[16,4096]{1,0:T(8,128)} custom-call(f32[16,4096]{1,0:T(8,128)} %dens_h.1, f32[3,4096]{1,0:T(4,128)} %pts_h.1, f32[16,128,128]{2,1,0:T(8,128)} %bitcast.5, f32[16,128,128]{2,1,0:T(8,128)} %bitcast.6, f32[8,16,128,128]{3,2,1,0:T(8,128)} %bitcast.4, s32[4,32]{1,0:T(4,128)} %bitcast.7, s32[32]{0:T(128)} %cnt_h.1), custom_call_target="tpu_custom_call" | custom-call | tf_op jit(solution)/shard_map/helmholtz/pallas_call | solution.py:336
  48.2 1.7 %copy.9 = f32[16,4096]{1,0:T(8,128)} copy(f32[16,4096]{1,0:T(8,128)} %helmholtz.1) | data formatting | bytes 524288

commit v2 on v1

--- a/solution.py
+++ b/solution.py
@@ -20,6 +20,8 @@
 RANK = 64
 PAD = 2
 CHUNKS = 4
+FIRST = (1, 3, 3, 4, 3, 3, 3)
+SECOND = (3, 4, 4, 4, 2, 2, 1)
 
 
 def fit(func, degree, low, high):
@@ -82,14 +84,22 @@
 
 
 def level_pair(own, part, mats):
-    x = jnp.concatenate([own, part], axis=0)
-    low = lane_low((2 * RHS, 128))
-    zero = jnp.zeros_like(x)
-    x = tall(jnp.concatenate([jnp.where(low, x, zero), jnp.where(low, zero, x)], axis=0))
-    a = fold(jnp.dot(x, wide(mats), preferred_element_type=F32), 4 * RHS)
-    own0, part0, own1, part1 = (a[i * RHS : (i + 1) * RHS] for i in range(4))
+    hi, lo = split2(jnp.concatenate([own, part], axis=0))
+    x = jnp.concatenate(
+        [jnp.concatenate([hi, hi], axis=1), jnp.concatenate([lo, jnp.zeros_like(lo)], axis=1)], axis=0
+    )
+    zero = jnp.zeros((RANK, 128), BF16)
+
+    def diagonal(m):
+        top = jnp.concatenate([m[:RANK], zero], axis=0)
+        return jnp.concatenate([top, jnp.concatenate([zero, m[RANK:]], axis=0)], axis=1)
+
+    weights = jnp.concatenate([diagonal(m) for m in split2(mats)], axis=0)
+    r = jnp.dot(x, weights, preferred_element_type=F32)
+    a = r[: 2 * RHS] + r[2 * RHS :]
     low = lane_low((RHS, 128))
-    return jnp.where(low, own0, part1) + pltpu.roll(jnp.where(low, own1, part0), RANK, 1)
+    kept = jnp.where(low, a[:RHS, :128], a[RHS:, 128:])
+    return kept + pltpu.roll(jnp.where(low, a[:RHS, 128:], a[RHS:, :128]), RANK, 1)
 
 
 def interp_pair(state, mats):
@@ -109,9 +119,9 @@
 
 def kernel(
     n_hi, n_lo, leaves,
-    dens_h, pts_h, basis_h, interp_h, trans_h, off_h, cnt_h, out_ref,
-    dens, pts, basis, interp, trans, off, cnt, nxt, halo_d, halo_p, own, part, feat, coords, srcs, items,
-    in_sem, basis_sem, trans_sem, send_sem, recv_sem, halo_send, halo_recv,
+    dens_h, pts_h, basis_h, interp_h, trans_h, off_h, cnt_h, out_h, near_h,
+    dens, pts, basis, interp, trans, off, cnt, nxt, halo_d, halo_p, own, part, feat, coords, srcs, items, out_ref, near_ref,
+    in_sem, basis_sem, trans_sem, send_sem, recv_sem, halo_send, halo_recv, out_sem, near_sem,
 ):
     levels, pairs = trans.shape[0], trans.shape[1]
     per = pairs // CHUNKS
@@ -151,13 +161,7 @@
     load_dens.start()
     for copy in load_basis:
         copy.start()
-    load_trans(0).start()
     load_pts.start()
-    load_off.start()
-    load_cnt.start()
-    for level in range(1, levels):
-        load_trans(level).start()
-    load_interp.start()
 
     def send(level, chunk, target):
         return pltpu.make_async_remote_copy(
@@ -196,23 +200,28 @@
             return 0
 
         lax.fori_loop(0, per, coef_step, 0, unroll=True)
+        if c == 0:
+            pl.semaphore_wait(barrier, levels + 2)
+        send(0, c, partner(1)).start()
+    load_off.start()
+    load_cnt.start()
+    for level in range(levels):
+        load_trans(level).start()
+    load_interp.start()
     load_pts.wait()
-    pl.semaphore_wait(barrier, levels + 2)
-    for c in range(CHUNKS):
-        send(0, c, partner(1)).start()
     for copy in halo_copies:
         copy.start()
 
     def level_task(level, chunk):
-        for i in range(per):
-            p = chunk * per + i
-            own[level + 1, p] = level_pair(own[level, p], part[level, p], trans[level, p])
+        places = [chunk * per + i for i in range(per)]
+        return [level_pair(own[level, p], part[level, p], trans[level, p]) for p in places]
 
     load_trans(0).wait()
 
     def first_task(chunk, _):
         send(0, chunk, partner(1)).wait()
-        level_task(0, chunk)
+        for i, out in enumerate(level_task(0, chunk)):
+            own[1, chunk * per + i] = out
         send(1, chunk, partner(2)).start()
         return 0
 
@@ -271,55 +280,80 @@
         done = slot >= cnt[leaf]
         return jnp.where(done, nxt[leaf + 1], leaf), jnp.where(done, 0, slot), acc
 
-    def unit(k, carry):
-        leaf, slot, acc = carry
-        for i in range(2):
-            leaf, slot, acc = item(2 * k + i, leaf, slot, acc)
-        return leaf, slot, acc
-
-    units = items.shape[0] // 2
-    every = units // ((levels - 1) * CHUNKS)
-    spare = units - every * (levels - 1) * CHUNKS
-    carry = (first_leaf, jnp.int32(0), jnp.zeros((RHS, LEAF), F32))
-    carry = lax.fori_loop(0, spare, unit, carry)
+    total_items = items.shape[0]
+    last = levels - 1
+
+    def fill(level, chunk, state):
+        n = jnp.int32(0)
+        for i, (first, second) in enumerate(zip(FIRST, SECOND)):
+            n = jnp.where(level == i + 1, jnp.where(lo % 2 == 0, first, second), n)
+        n = jnp.where(chunk == 0, n, 0)
+
+        def body(_, state):
+            return one(one(state))
+
+        return lax.fori_loop(0, n, body, state)
+
+    def one(state):
+        k, leaf, slot, acc = state
+        return (k + 1, *item(k, leaf, slot, acc))
 
     def middle_level(level, state):
-        bit, carry = state
+        bit, state = state
         load_trans(level).wait()
 
-        def task(chunk, carry):
-            start = spare + ((level - 1) * CHUNKS + chunk) * every
-            carry = lax.fori_loop(start, start + every, unit, carry)
+        def task(chunk, state):
+            state = fill(level, chunk, state)
             send(level, chunk, partner(bit)).wait()
-            level_task(level, chunk)
+            outs = level_task(level, chunk)
+            state = one(state)
+            for i, out in enumerate(outs):
+                own[level + 1, chunk * per + i] = out
             send(level + 1, chunk, partner(bit * 2)).start()
-            return carry
-
-        return bit * 2, lax.fori_loop(0, CHUNKS, task, carry)
-
-    bit, carry = lax.fori_loop(1, levels - 1, middle_level, (jnp.int32(2), carry))
-    last = levels - 1
-    for chunk in range(CHUNKS):
-        start = spare + ((last - 1) * CHUNKS + chunk) * every
-        carry = lax.fori_loop(start, start + every, unit, carry)
+            return state
+
+        return bit * 2, lax.fori_loop(0, CHUNKS, task, state)
+
+    state = (jnp.int32(0), first_leaf, jnp.int32(0), jnp.zeros((RHS, LEAF), F32))
+    bit, state = lax.fori_loop(1, last, middle_level, (jnp.int32(2), state))
+    done = [CHUNKS * (levels - 2) + 2 * sum(t[: levels - 2]) for t in (FIRST, SECOND)]
+    rest = jnp.where(lo % 2 == 0, *[(total_items - d) // 2 for d in done])
+    lax.fori_loop(0, rest, lambda _, state: one(one(state)), state)
+    def gather(q, end):
+        count = cnt[q]
+        end = end + count
+        near = jnp.where(count > 0, items[jnp.maximum(end - 1, 0)], 0.0)
+        near_ref[:, pl.ds(pl.multiple_of(q * LEAF, LEAF), LEAF)] = near
+        return end
+
+    lax.fori_loop(0, leaves, gather, jnp.int32(0), unroll=4)
+    store_near = pltpu.make_async_copy(near_ref, near_h, near_sem.at[0])
+    store_near.start()
     load_trans(last).wait()
     load_interp.wait()
 
-    def last_task(chunk, end):
+    def store_out(chunk):
+        columns = pl.ds(chunk * per * 2 * LEAF, per * 2 * LEAF)
+        if not isinstance(chunk, int):
+            columns = pl.ds(pl.multiple_of(chunk * per * 2 * LEAF, LEAF), per * 2 * LEAF)
+        return pltpu.make_async_copy(out_ref.at[:, columns], out_h.at[:, columns], out_sem.at[chunk])
+
+    def last_task(chunk, _):
         send(last, chunk, partner(1 << last)).wait()
-        level_task(last, chunk)
+        outs = level_task(last, chunk)
         for i in range(per):
             p = chunk * per + i
-            far = interp_pair(own[levels, p], interp[p])
+            far = interp_pair(outs[i], interp[p])
             for h in range(2):
-                q = 2 * p + h
-                count = cnt[q]
-                end = end + count
-                near = jnp.where(count > 0, items[jnp.maximum(end - 1, 0)], 0.0)
-                out_ref[:, pl.ds(pl.multiple_of(q * LEAF, LEAF), LEAF)] = far[h * RHS : (h + 1) * RHS] + near
-        return end
-
-    lax.fori_loop(0, CHUNKS, last_task, jnp.int32(0))
+                base = pl.multiple_of((2 * p + h) * LEAF, LEAF)
+                out_ref[:, pl.ds(base, LEAF)] = far[h * RHS : (h + 1) * RHS]
+        store_out(chunk).start()
+        return 0
+
+    lax.fori_loop(0, CHUNKS, last_task, 0)
+    store_near.wait()
+    for chunk in range(CHUNKS):
+        store_out(chunk).wait()
 
 
 def solution(mesh):
@@ -333,11 +367,11 @@
         capacity = leaves * offsets.shape[1] // 2
         any_spec = pl.BlockSpec(memory_space=pl.ANY)
         dma = pltpu.SemaphoreType.DMA
-        return pl.pallas_call(
+        far, near = pl.pallas_call(
             functools.partial(kernel, n_hi, n_lo, leaves),
-            out_shape=jax.ShapeDtypeStruct(density.shape, F32),
+            out_shape=[jax.ShapeDtypeStruct(density.shape, F32)] * 2,
             in_specs=[any_spec] * 7,
-            out_specs=pl.BlockSpec(memory_space=pltpu.VMEM),
+            out_specs=[any_spec] * 2,
             scratch_shapes=[
                 pltpu.VMEM(density.shape, F32),
                 pltpu.VMEM(points.shape, F32),
@@ -349,12 +383,14 @@
                 pltpu.SMEM((leaves + 1,), jnp.int32),
                 pltpu.VMEM((2, RHS, PAD * LEAF), F32),
                 pltpu.VMEM((2, 3, PAD * LEAF), F32),
-                pltpu.VMEM((levels + 1, pairs, RHS, 128), F32),
+                pltpu.VMEM((levels, pairs, RHS, 128), F32),
                 pltpu.VMEM((levels, pairs, RHS, 128), F32),
                 pltpu.VMEM((ext, LEAF, 48), BF16),
                 pltpu.VMEM((ext, 8, LEAF), F32),
                 pltpu.VMEM((ext, 2 * RHS, 2 * LEAF), BF16),
                 pltpu.VMEM((capacity, RHS, LEAF), F32),
+                pltpu.VMEM(density.shape, F32),
+                pltpu.VMEM(density.shape, F32),
                 dma((5,)),
                 dma((CHUNKS,)),
                 dma((levels,)),
@@ -362,6 +398,8 @@
                 dma((levels, CHUNKS)),
                 dma((4,)),
                 dma((4,)),
+                dma((CHUNKS,)),
+                dma((1,)),
             ],
             compiler_params=pltpu.CompilerParams(
                 collective_id=0, has_side_effects=True, vmem_limit_bytes=60 << 20
@@ -376,6 +414,7 @@
             offsets.T,
             counts,
         )
+        return far + near
 
     return jax.shard_map(
         shards,

time: 50 us -> 49.3 us (0.986)
  other arithmetic: 0 us -> 1.76 us
  local copies, waits for them, and re-layouts: 1.67 us -> 0 us
  Pallas kernels: 48.2 us -> 47.4 us
    add x0 -> x1, other arithmetic: none -> 1.76 us  [shards(): return far + near]
    unnamed x1 -> x0, local copies, waits for them, and re-layouts: 1.67 us -> none
    pallas_call x1, Pallas kernels: 48.2 us -> 47.4 us  [shards(): pl.pallas_call(functools.partial(kernel, n_hi, n_lo, leaves), out_shape=[...]
where the time goes in v2:
time: 49.3 us; the launch traced here: 49.1 us
  Pallas kernels  47.4 us (96%)
  other arithmetic  1.76 us (4%)
    pallas_call x1, Pallas kernels, shards(): pl.pallas_call(functools.partial(kernel, n_hi, n_lo, leaves), out_shape=[...  47.4 us
    add x1, other arithmetic, shards(): return far + near  1.76 us

profile of v2, /device:TPU:16, one launch (start us, length us, event | category | flops | bytes accessed | tf_op | source)
XLA Modules:
  0.0 49.1 jit_solution(18259899445896577761)
XLA Ops:
  0.0 47.4 %helmholtz.1 = (f32[16,4096]{1,0:T(8,128)}, f32[16,4096]{1,0:T(8,128)}) custom-call(f32[16,4096]{1,0:T(8,128)} %dens_h.1, f32[3,4096]{1,0:T(4,128)} %pts_h.1, f32[16,128,128]{2,1,0:T(8,128)} %bitcast.5, f32[16,128,128]{2,1,0:T(8,128)} %bitcast.6, f32[8,16,128,128]{3,2,1,0:T(8,128)} %bitcast.4, s32[4,32]{1,0:T(4,128)} %bitcast.7, s32[32]{0:T(128)} %cnt_h.1), custom_call_target="tpu_custom_call" | custom-call | tf_op jit(solution)/shard_map/helmholtz/pallas_call | solution.py:370
  47.4 1.8 %add.3 = f32[16,4096]{1,0:T(8,128)} add(f32[16,4096]{1,0:T(8,128)} %get-tuple-element.7, f32[16,4096]{1,0:T(8,128)} %get-tuple-element.8) | non-fusion elementwise | flops 65536 | bytes 786432 | tf_op jit(solution)/shard_map/add | solution.py:417

commit v3 on v2

--- a/solution.py
+++ b/solution.py
@@ -21,7 +21,7 @@
 PAD = 2
 CHUNKS = 4
 FIRST = (1, 3, 3, 4, 3, 3, 3)
-SECOND = (3, 4, 4, 4, 2, 2, 1)
+SECOND = (5, 5, 5, 4, 1, 0, 0)
 
 
 def fit(func, degree, low, high):

time: 49.3 us -> 48.6 us (0.986)
  Pallas kernels: 47.4 us -> 46.5 us
    pallas_call x1, Pallas kernels: 47.4 us -> 46.5 us  [shards(): pl.pallas_call(functools.partial(kernel, n_hi, n_lo, leaves), out_shape=[...]
where the time goes in v3:
time: 48.6 us; the launch traced here: 48.3 us
  Pallas kernels  46.5 us (96%)
  other arithmetic  1.76 us (4%)
    pallas_call x1, Pallas kernels, shards(): pl.pallas_call(functools.partial(kernel, n_hi, n_lo, leaves), out_shape=[...  46.5 us
    add x1, other arithmetic, shards(): return far + near  1.76 us

profile of v3, /device:TPU:16, one launch (start us, length us, event | category | flops | bytes accessed | tf_op | source)
XLA Modules:
  0.0 48.3 jit_solution(13718236938417575046)
XLA Ops:
  0.0 46.5 %helmholtz.1 = (f32[16,4096]{1,0:T(8,128)}, f32[16,4096]{1,0:T(8,128)}) custom-call(f32[16,4096]{1,0:T(8,128)} %dens_h.1, f32[3,4096]{1,0:T(4,128)} %pts_h.1, f32[16,128,128]{2,1,0:T(8,128)} %bitcast.5, f32[16,128,128]{2,1,0:T(8,128)} %bitcast.6, f32[8,16,128,128]{3,2,1,0:T(8,128)} %bitcast.4, s32[4,32]{1,0:T(4,128)} %bitcast.7, s32[32]{0:T(128)} %cnt_h.1), custom_call_target="tpu_custom_call" | custom-call | tf_op jit(solution)/shard_map/helmholtz/pallas_call | solution.py:370
  46.6 1.8 %add.3 = f32[16,4096]{1,0:T(8,128)} add(f32[16,4096]{1,0:T(8,128)} %get-tuple-element.7, f32[16,4096]{1,0:T(8,128)} %get-tuple-element.8) | non-fusion elementwise | flops 65536 | bytes 786432 | tf_op jit(solution)/shard_map/add | solution.py:417
